TPU v7x, 512 devices: a whole 4x4x16 slice. The times are simulated.
512 devices in a mesh: dp: 8 (over x, core), vocab: 64 (over z, y).
Axes of the slice: x: 4, y: 4, z: 16, core: 2. Of those that a mesh axis runs over, the one named last changes fastest.
Arguments:
- hidden_states: bfloat16 [1024, 4096], P('dp'), may hold values from -6 to 6
- head_weight: bfloat16 [4096, 65536], P('dp', 'vocab'), may hold values from -4 to 4
- teacher_index: int32 [1024, 64], P(('dp', 'vocab')), may hold values from 0 to 65535, as said below
- teacher_logits: float32 [1024, 64], P(('dp', 'vocab')), may hold values from -12 to 312
- loss_weight: float32 [1024], P('dp'), may hold values from 8 to 64
Outputs:
- head_grad: bfloat16 [4096, 65536], P('dp', 'vocab')
- hidden_grad: bfloat16 [1024, 4096], P('dp', 'vocab')
Inputs may be any that keep to these rules, and one draw needn't show every extreme that they name: `teacher_index`: each row names 64 different entries.
All inputs are finite; a program needn't handle non-finite values.
Results may differ from a plain program's by a relative error of at most 0.0085.
Values may be sent and summed in bfloat16 or wider, within the bound.
A program may use at most 64 MiB of HBM per device.

v0:
```python
import jax
import jax.numpy as jnp
from jax import lax
from jax.sharding import PartitionSpec as P


def local(hidden_states, head_weight, teacher_index, teacher_logits, loss_weight):
    shard = head_weight.shape[1]
    vocab_start = lax.axis_index("vocab") * shard
    full_weight = lax.all_gather(head_weight, "dp", axis=0, tiled=True)
    logits = jnp.dot(hidden_states, full_weight, preferred_element_type=jnp.float32)
    local_top = jnp.max(logits, axis=1)
    top = lax.pmax(local_top, "vocab")
    total = lax.psum(jnp.sum(jnp.exp(logits - top[:, None]), axis=1), "vocab")
    student = jnp.exp(logits - top[:, None]) / total[:, None]
    teacher_top = jnp.max(teacher_logits, axis=1, keepdims=True)
    teacher_exp = jnp.exp(teacher_logits - teacher_top)
    target_weight = teacher_exp / jnp.sum(teacher_exp, axis=1, keepdims=True)
    all_index, all_weight = (
        lax.all_gather(teacher_index, "vocab", axis=0, tiled=True),
        lax.all_gather(target_weight, "vocab", axis=0, tiled=True),
    )
    offsets = all_index - vocab_start
    inside = (offsets >= 0) & (offsets < shard)
    columns = jnp.where(inside, offsets, shard)
    row_ids = jnp.broadcast_to(
        jnp.arange(all_index.shape[0], dtype=jnp.int32)[:, None], all_index.shape
    )
    dense_target = (
        jnp.zeros((all_index.shape[0], shard), jnp.float32)
        .at[row_ids, columns]
        .add(all_weight, mode="drop")
    )
    grad_logits = (loss_weight[:, None] * (student - dense_target)).astype(jnp.bfloat16)
    terms = lax.dot_general(
        grad_logits, full_weight, (((1,), (1,)), ((), ())), preferred_element_type=jnp.float32
    )
    hidden_grad = lax.psum_scatter(terms, "vocab", scatter_dimension=1, tiled=True).astype(
        jnp.bfloat16
    )
    features = lax.all_to_all(hidden_states, "dp", split_axis=1, concat_axis=0, tiled=True)
    head_grad = lax.dot_general(
        features,
        lax.all_gather(grad_logits, "dp", axis=0, tiled=True),
        (((0,), (0,)), ((), ())),
        preferred_element_type=jnp.float32,
    ).astype(jnp.bfloat16)
    return (head_grad, hidden_grad)


def solution(mesh):
    in_specs = (
        P("dp", None),
        P("dp", "vocab"),
        P(("dp", "vocab"), None),
        P(("dp", "vocab"), None),
        P("dp"),
    )
    out_specs = (P("dp", "vocab"), P("dp", "vocab"))
    return jax.shard_map(local, mesh=mesh, in_specs=in_specs, out_specs=out_specs, check_vma=False)
```

profile of v0, /device:TPU:2, one launch (start us, length us, event | category | flops | bytes accessed | tf_op | source)
XLA Modules:
  0.0 1232.3 jit_solution(15792176934259515390)
XLA Ops:
  7.2 0.7 all-gather.5.cloned.1.call-update
  7.9 0.8 reduce_max.19
  8.7 0.9 fusion.5
  9.6 0.8 divide_bitcast_fusion
  10.4 88.6 %all-gather.1 = f32[64,2,64]{2,1,0:T(2,128)S(1)} all-gather(f32[1,2,64]{2,1,0:T(2,128)S(1)} %divide_bitcast_fusion), channel_id=1, replica_groups=mesh['dp'=8,'vocab'=64] {'vocab'}, dimensions={0}, use_global_device_ids=true | all-gather | bytes 33280 | tf_op jit(solution)/shard_map/all_gather | solution.py:21
  98.9 0.1 reshape.30
  99.0 80.5 %all-gather = s32[64,2,64]{2,1,0:T(2,128)S(1)} all-gather(s32[1,2,64]{2,1,0:T(2,128)} %bitcast.24), channel_id=1, replica_groups=mesh['dp'=8,'vocab'=64] {'vocab'}, dimensions={0}, use_global_device_ids=true | all-gather | bytes 33280 | tf_op jit(solution)/shard_map/all_gather | solution.py:20
  179.6 0.7 multiply_reduce_fusion
  180.4 0.8 and_reduce_fusion
  181.2 44.1 %scatter_custom_fusion = f32[131072]{0:T(1024)S(1)} fusion(s32[8192]{0:T(1024)S(1)} %reshape.28, f32[8192]{0:T(1024)S(1)} %reshape.30, f32[]{:T(128)} %constant.6.clone.1), kind=kCustom, calls=%fused_computation.6 | custom fusion | flops 8192 | bytes 524292
  225.3 0.1 reshape.27
  225.4 5.1 fusion.6
  230.5 140.2 %pmax.7 = f32[128]{0:T(128)S(1)} all-reduce(f32[128]{0:T(128)S(1)} %get-tuple-element.10), channel_id=1, replica_groups=mesh['dp'=8,'vocab'=64] {'vocab'}, use_global_device_ids=true, to_apply=%region_1.0 | all-reduce | flops 128 | bytes 1024 | tf_op jit(solution)/shard_map/pmax | solution.py:13
  370.7 0.2 fusion.1
  370.9 138.0 %psum.7 = f32[128]{0:T(128)S(1)} all-reduce(f32[128]{0:T(128)S(1)} %fusion.1), channel_id=1, replica_groups=mesh['dp'=8,'vocab'=64] {'vocab'}, use_global_device_ids=true, to_apply=%region_3.0 | all-reduce | flops 128 | bytes 1024 | tf_op jit(solution)/shard_map/psum | solution.py:14
  508.9 0.9 multiply_convert_fusion
  509.9 7.1 fusion.7
  517.0 0.7 copy.12
  517.7 27.3 %all_to_all.19 = bf16[128,8,512]{0,2,1:T(8,128)(2,1)S(1)} all-to-all(bf16[128,8,512]{0,2,1:T(8,128)(2,1)S(1)} %bitcast.20), channel_id=1, replica_groups=mesh['dp'=8,'vocab'=64] {'dp'}, dimensions={1} | all-to-all | bytes 2097152 | tf_op jit(solution)/shard_map/all_to_all | solution.py:41
  545.0 0.5 copy.13
  545.6 2.9 fusion
  548.5 1.3 copy.14
  549.8 674.6 %reduce-scatter.2.cloned.1.call-done = f32[128,64]{0,1:T(8,128)} async-done(((f32[128,4096]{0,1:T(8,128)}), f32[128,64]{0,1:T(8,128)}) %reduce-scatter.2.cloned.1.call-update) | async-done | bytes 32784 | tf_op jit(solution)/shard_map/reduce_scatter | solution.py:38
  1224.4 1.4 convert_element_type.15
  (16 shorter events, 0.3 us)
Async XLA Ops:
  7.2 218.3 %all-gather.5.cloned.1.call-start = ((), (), s32[]{:S(2)}) async-start(), calls=%async_computation.2 | async-start | bytes 9437184 | tf_op jit(solution)/shard_map/all_gather | solution.py:10
  7.9 537.7 %all-gather.7.cloned.1.call-start = ((), (), s32[]{:S(2)}) async-start(), calls=%async_computation.3 | async-start | bytes 2359296 | tf_op jit(solution)/shard_map/all_gather | solution.py:44
  225.4 283.5 %copy-start.1 = (f32[128]{0:T(128)S(1)}, f32[128]{0:T(128)}, u32[]{:S(2)}) copy-start(f32[128]{0:T(128)} %param.9) | copy-start | bytes 1540
  230.5 286.5 %copy-start = (bf16[128,4096]{1,0:T(8,128)(2,1)S(1)}, bf16[128,4096]{1,0:T(8,128)(2,1)}, u32[]{:S(2)}) copy-start(bf16[128,4096]{1,0:T(8,128)(2,1)} %param.5) | copy-start | bytes 3145732
  509.8 714.6 %reduce-scatter.2.cloned.1.call-start = ((), (), s32[]{:S(2)}) async-start(), calls=%async_computation.4 | async-start | bytes 2129920 | tf_op jit(solution)/shard_map/reduce_scatter | solution.py:38
Sparse Core Ops, SparseCore 0:
  10.1 61.0 all-gather.4
  509.9 35.0 all-gather.6
  549.4 674.9 reduce-scatter.1
where the time goes:
time: 1230 us
  waiting for transfers between devices  675 us (55%)
  blocking collectives  475 us (39%)
  other arithmetic  50.5 us (4%)
  matrix products  15 us (1%)
  between operations  13.9 us (1%)
    reduce_scatter x1, waiting for transfers between devices, local(): lax.psum_scatter(terms, 'vocab', scatter_dimension=1, tiled=True)  675 us
    pmax x1, blocking collectives, local(): top = lax.pmax(local_top, 'vocab')  140 us
    psum x1, blocking collectives, local(): total = lax.psum(jnp.sum(jnp.exp(logits - top[:, None]), axis=1), 'vocab')  138 us
    all_gather x1, blocking collectives, local(): lax.all_gather(target_weight, 'vocab', axis=0, tiled=True)  88.6 us
    all_gather x1, blocking collectives, local(): lax.all_gather(teacher_index, 'vocab', axis=0, tiled=True)  80.5 us
    unnamed x5, other arithmetic  46.4 us
    all_to_all x1, blocking collectives, local(): lax.all_to_all(hidden_states, 'dp', split_axis=1, concat_axis=0, tiled=True)  27.3 us
  transfers between devices with their start and end apart: 3, of which 1 were waited for; matrix products, arithmetic and copies ran while one was open for 5% of the time, Pallas kernels for 0%

commit v1 on v0

v1 whole, which is shorter than its diff:
```python
import functools

import jax
import jax.numpy as jnp
from jax import lax
from jax.experimental import pallas as pl
from jax.experimental.pallas import tpu as pltpu
from jax.sharding import PartitionSpec as P

MESH = pl.DeviceIdType.MESH
F32 = jnp.float32
BF16 = jnp.bfloat16

NX, NY, NZ = 4, 4, 16
TOK = 128
D = 4096
DX = D // NX
DC = DX // 2
V = 1024
ZZ = NZ // NX
DZ = DX // ZZ
DY = DZ // NY
K = 64
HD = F32


def dot(a, b, ca, cb):
    return lax.dot_general(a, b, (((ca,), (cb,)), ((), ())), preferred_element_type=F32)


def kernel(
    h, w, ti, tl, lw, head_o, hid_o,
    wn, wt, feat, feat_o, feat_t, part, fin_l, rel_l, tgt, g, go,
    hf, hs, yrel, yfin, yred, fin, tea, tez, tet, sty, stz, fin_keep,
    ss, rs, ls, fs, fr,
):
    dp, vo = lax.axis_index("dp"), lax.axis_index("vocab")
    x, c = dp // 2, dp % 2
    z, y = vo // NY, vo % NY
    xp, x2, xm = (x + 1) % NX, (x + 2) % NX, (x + 3) % NX
    yp, y2, ym = (y + 1) % NY, (y + 2) % NY, (y + 3) % NY

    def at(xx, cc, zz, yy):
        return (xx * 2 + cc, zz * NY + yy)

    to_x = [None] + [at((x + r) % NX, c, z, y) for r in range(1, NX)]
    to_y = [None] + [at(x, c, z, (y + r) % NY) for r in range(1, NY)]
    to_z = [None] + [at(x, c, (z + r) % NZ, y) for r in range(1, NZ)]
    mate = at(x, 1 - c, z, y)

    count = [0]
    sent = []

    def send(src, dst, dev):
        i = count[0]
        count[0] += 1
        d = pltpu.make_async_remote_copy(src, dst, ss.at[i], rs.at[i], device_id=dev, device_id_type=MESH)
        d.start()
        sent.append(d)
        return d

    own_w = pltpu.make_async_copy(w, wn.at[c], ls.at[0])
    own_w.start()
    own_h = pltpu.make_async_copy(h.at[:, pl.ds(pl.multiple_of(x * DX, DX), DX)], feat.at[0], ls.at[1])
    own_h.start()

    barrier = pltpu.get_barrier_semaphore()
    peers = to_x[1:] + [mate] + to_y[1:] + to_z[1:]
    for dev in peers:
        pl.semaphore_signal(barrier, inc=1, device_id=dev, device_id_type=MESH)
    pl.semaphore_wait(barrier, len(peers))

    d_feat = [None] * NX
    for r in (2, 1, 3):
        xx = (x + r) % NX
        d_feat[NX - r] = send(h.at[:, pl.ds(pl.multiple_of(xx * DX, DX), DX)], feat.at[NX - r], to_x[r])
    d_w = send(w, wn.at[c], mate)

    row = lax.broadcasted_iota(jnp.int32, (8, 128), 0)
    mine = jnp.concatenate([ti[...].astype(F32), tl[...]], axis=1)
    mine = jnp.concatenate([mine] * 4, axis=0)
    tea[0] = jnp.where(row // 2 == y, mine, 0.0)
    d_tea = [send(tea.at[0], tea.at[NY - r], to_y[r]) for r in range(1, NY)]

    def transpose_w(core):
        def body(i, carry):
            rows = pl.ds(pl.multiple_of(i * 128, 128), 128)
            wt[rows, pl.ds(pl.multiple_of(core * DC, DC), DC)] = wn[core, :, rows].T
            return carry

        lax.fori_loop(0, V // 128, body, 0)

    own_w.wait()
    transpose_w(c)
    own_h.wait()
    for d in d_tea:
        d.wait_recv()
    tez[0] = tea[0] + tea[1] + tea[2] + tea[3]
    d_tez = [send(tez.at[0], tez.at[NZ - r], to_z[r]) for r in range(1, NZ)]
    d_w.wait_recv()
    transpose_w(1 - c)

    def partial(r, lo, hi):
        def body(i, carry):
            rows = pl.ds(pl.multiple_of(i * 256, 256), 256)
            part[r, rows, :] = dot(wt[rows, :], feat[r], 1, 1)
            return carry

        lax.fori_loop(lo // 256, hi // 256, body, 0)

    half = V // 2
    top, bot = pl.ds(0, half), pl.ds(half, half)
    d_feat[2].wait_recv()
    partial(2, 0, V)
    r_top = send(part.at[2, top], rel_l.at[0], to_x[3])
    r_bot = send(part.at[2, bot], rel_l.at[1], to_x[1])
    d_feat[1].wait_recv()
    partial(1, 0, V)
    a_p = send(part.at[1, top], fin_l.at[0, top], to_x[1])
    d_feat[3].wait_recv()
    partial(3, 0, V)
    a_m = send(part.at[3, bot], fin_l.at[1, bot], to_x[3])
    d_fo = []
    for r in (0, 2, 1, 3):
        cols = pl.ds(pl.multiple_of((1 - c) * DC, DC), DC)
        d_fo.append(send(feat.at[r, :, cols], feat_o.at[r], mate))
    r_bot.wait_recv()
    part[1, bot, :] += rel_l[1]
    b_p = send(part.at[1, bot], fin_l.at[0, bot], to_x[1])
    r_top.wait_recv()
    part[3, top, :] += rel_l[0]
    b_m = send(part.at[3, top], fin_l.at[1, top], to_x[3])
    partial(0, 0, V)

    for d in d_tez:
        d.wait_recv()
    for r in range(NZ):
        tet[pl.ds(pl.multiple_of(((z + r) % NZ) * 8, 8), 8), :] = tez[r]
    tt = tet[...].T
    tlog = tt[K:, :]
    texp = jnp.exp(tlog - jnp.max(tlog, axis=0, keepdims=True))
    lwr = lw[...].reshape(1, TOK)
    tet[pl.ds(K, K), :] = texp / jnp.sum(texp, axis=0, keepdims=True) * lwr
    tet[pl.ds(0, K), :] = tt[:K, :] - (vo * V).astype(F32)

    def dense(i, carry):
        base = pl.multiple_of(i * 128, 128)
        at_row = (lax.broadcasted_iota(jnp.int32, (128, TOK), 0) + base).astype(F32)
        acc = jnp.zeros((128, TOK), F32)
        for k in range(K):
            acc = jnp.where(at_row == tet[k : k + 1, :], tet[K + k : K + k + 1, :], acc)
        tgt[pl.ds(base, 128), :] = acc
        return carry

    lax.fori_loop(0, V // 128, dense, 0)

    own_cols = pl.ds(pl.multiple_of(c * DC, DC), DC)
    for r in range(NX):
        feat_t[r] = feat[r, :, own_cols].T
    for d in d_fo:
        d.wait_recv()
    for r in range(NX):
        feat_t[NX + r] = feat_o[r].T

    for d in (a_p, a_m, b_p, b_m):
        d.wait_recv()
    logits = part[0] + (fin_l[0] + fin_l[1])
    m_loc = jnp.max(logits, axis=0, keepdims=True)
    p = jnp.exp(logits - m_loc)
    part[0] = p
    s_loc = jnp.sum(p, axis=0, keepdims=True)

    def exchange(buf, tos, m, s):
        n = len(tos)
        buf[0] = jnp.where(row == 0, m, s)
        ds = [send(buf.at[0], buf.at[n - r], tos[r]) for r in range(1, n)]
        for d in ds:
            d.wait_recv()
        ms = [buf[r, 0:1, :] for r in range(n)]
        mm = functools.reduce(jnp.maximum, ms)
        return mm, sum(buf[r, 1:2, :] * jnp.exp(ms[r] - mm) for r in range(n))

    m_y, s_y = exchange(sty, to_y, m_loc, s_loc)
    m_all, s_all = exchange(stz, to_z, m_y, s_y)
    scale = lwr * jnp.exp(m_loc - m_all) / s_all
    g[0] = (part[0] * scale - tgt[...]).astype(BF16)

    gp_b = send(g.at[0, bot], g.at[3, bot], to_x[1])
    gm_t = send(g.at[0, top], g.at[1, top], to_x[3])
    gp_t = send(g.at[0, top], g.at[3, top], to_x[1])
    gm_b = send(g.at[0, bot], g.at[1, bot], to_x[3])
    d_go = [send(g.at[0], go.at[0], mate)]

    hrow = DZ // 2 * 2
    ht, hb = pl.ds(0, hrow // 2), pl.ds(hrow // 2, hrow // 2)
    pieces = {}

    def hidden(r):
        for q in range(ZZ):
            rows = q * DZ
            v = dot(wn[rows // DC, rows % DC : rows % DC + DZ, :], g[r], 1, 0)
            for yy in range(NY):
                hf[r, yy, q * DY : (q + 1) * DY, :] = v[yy * DY : (yy + 1) * DY]
        if HD == F32:
            src = hf
        else:
            hs[r] = hf[r].astype(HD)
            src = hs
        rt = send(src.at[r, y2, ht], yrel.at[r, 0], to_y[3])
        rb = send(src.at[r, y2, hb], yrel.at[r, 1], to_y[1])
        pt = send(src.at[r, yp, ht], yfin.at[r, 0, ht], to_y[1])
        mb = send(src.at[r, ym, hb], yfin.at[r, 1, hb], to_y[3])
        pieces[r] = [rt, rb, pt, mb]

    def relay(r):
        src = hf if HD == F32 else hs
        rt, rb, pt, mb = pieces[r]
        rb.wait_recv()
        src[r, yp, hb, :] = (hf[r, yp, hb, :] + yrel[r, 1].astype(F32)).astype(HD)
        pb = send(src.at[r, yp, hb], yfin.at[r, 0, hb], to_y[1])
        rt.wait_recv()
        src[r, ym, ht, :] = (hf[r, ym, ht, :] + yrel[r, 0].astype(F32)).astype(HD)
        mt = send(src.at[r, ym, ht], yfin.at[r, 1, ht], to_y[3])
        pieces[r] = [pt, mb, pb, mt]

    fin_sent = []

    def finish(r):
        for d in pieces[r]:
            d.wait_recv()
        v = hf[r, y] + (yfin[r, 0].astype(F32) + yfin[r, 1].astype(F32))
        yred[r] = v.astype(HD)
        for q in range(ZZ):
            zd = x * ZZ + q
            i = r * ZZ + q
            d = pltpu.make_async_remote_copy(
                yred.at[r, pl.ds(q * DY, DY)], fin.at[z], fs.at[i], fr.at[z],
                device_id=at((x + r) % NX, c, zd, y), device_id_type=MESH,
            )
            if r == 0:
                fin_sent.append((d, zd != z))

                @pl.when(zd != z)
                def _(d=d):
                    d.start()

                @pl.when(zd == z)
                def _(q=q):
                    fin[z] = yred[0, q * DY : (q + 1) * DY, :]
            else:
                fin_sent.append((d, None))
                d.start()

    hidden(0)
    gp_b.wait_recv()
    g2_b = send(g.at[3, bot], g.at[2, bot], to_x[1])
    gm_t.wait_recv()
    g2_t = send(g.at[1, top], g.at[2, top], to_x[3])
    gp_t.wait_recv()
    d_go.append(send(g.at[3], go.at[3], mate))
    hidden(3)
    gm_b.wait_recv()
    d_go.append(send(g.at[1], go.at[1], mate))
    hidden(1)
    relay(0)
    relay(3)
    relay(1)
    g2_b.wait_recv()
    g2_t.wait_recv()
    d_go.append(send(g.at[2], go.at[2], mate))
    hidden(2)
    finish(0)
    finish(3)
    finish(1)
    relay(2)
    finish(2)

    for d in d_go:
        d.wait_recv()

    def head(i, carry):
        rows = pl.ds(pl.multiple_of(i // 4 * 256, 256), 256)
        cols = pl.ds(pl.multiple_of(i % 4 * 256, 256), 256)
        acc = dot(feat_t[0, rows, :], g[0, cols, :], 1, 1)
        for r in range(1, NX):
            acc += dot(feat_t[r, rows, :], g[r, cols, :], 1, 1)
        for r in range(NX):
            acc += dot(feat_t[NX + r, rows, :], go[r, cols, :], 1, 1)
        head_o[rows, cols] = acc.astype(BF16)
        return carry

    lax.fori_loop(0, (DC // 256) * (V // 256), head, 0)

    here = z // ZZ == x
    for zs in range(NZ):
        d = pltpu.make_async_remote_copy(
            yred.at[0, pl.ds(0, DY)], fin.at[zs], fs.at[0], fr.at[zs],
            device_id=mate, device_id_type=MESH,
        )

        @pl.when(jnp.logical_not(here & (z == zs)))
        def _(d=d):
            d.wait_recv()

    total = fin[0].astype(F32)
    for zs in range(1, NZ):
        total += fin[zs].astype(F32)
    fin_keep[pl.ds(0, DY), :] = total
    fin_keep[pl.ds(DY, DY), :] = jnp.zeros((DY, TOK), F32)
    hid_o[...] = fin_keep[...].T[:, :DY].astype(BF16)

    for d in sent:
        d.wait_send()
    for d, cond in fin_sent:
        if cond is None:
            d.wait_send()
        else:

            @pl.when(cond)
            def _(d=d):
                d.wait_send()


def local(hidden_states, head_weight, teacher_index, teacher_logits, loss_weight):
    vm = pl.BlockSpec(memory_space=pltpu.VMEM)
    anym = pl.BlockSpec(memory_space=pl.ANY)
    n_sems = 128
    scratch = [
        pltpu.VMEM((2, DC, V), BF16),
        pltpu.VMEM((V, DX), BF16),
        pltpu.VMEM((NX, TOK, DX), BF16),
        pltpu.VMEM((NX, TOK, DC), BF16),
        pltpu.VMEM((2 * NX, DC, TOK), BF16),
        pltpu.VMEM((NX, V, TOK), F32),
        pltpu.VMEM((2, V, TOK), F32),
        pltpu.VMEM((2, V // 2, TOK), F32),
        pltpu.VMEM((V, TOK), F32),
        pltpu.VMEM((NX, V, TOK), BF16),
        pltpu.VMEM((NX, V, TOK), BF16),
        pltpu.VMEM((NX, NY, DZ, TOK), F32),
        pltpu.VMEM((NX, NY, DZ, TOK) if HD != F32 else (1, 1, 8, TOK), HD),
        pltpu.VMEM((NX, 2, DZ // 2, TOK), HD),
        pltpu.VMEM((NX, 2, DZ, TOK), HD),
        pltpu.VMEM((NX, DZ, TOK), HD),
        pltpu.VMEM((NZ, DY, TOK), HD),
        pltpu.VMEM((NY, 8, 128), F32),
        pltpu.VMEM((NZ, 8, 128), F32),
        pltpu.VMEM((128, 128), F32),
        pltpu.VMEM((NY, 8, 128), F32),
        pltpu.VMEM((NZ, 8, 128), F32),
        pltpu.VMEM((128, 128), F32),
        pltpu.SemaphoreType.DMA((n_sems,)),
        pltpu.SemaphoreType.DMA((n_sems,)),
        pltpu.SemaphoreType.DMA((2,)),
        pltpu.SemaphoreType.DMA((NZ,)),
        pltpu.SemaphoreType.DMA((NZ,)),
    ]
    return pl.pallas_call(
        kernel,
        out_shape=(
            jax.ShapeDtypeStruct((DC, V), BF16),
            jax.ShapeDtypeStruct((TOK, DY), BF16),
        ),
        in_specs=[anym, anym, vm, vm, vm],
        out_specs=(vm, vm),
        scratch_shapes=scratch,
        compiler_params=pltpu.CompilerParams(
            collective_id=0, has_side_effects=True, vmem_limit_bytes=56 * 1024 * 1024
        ),
        cost_estimate=pl.CostEstimate(flops=3 * 2 * 128 * 4096 * 1024, bytes_accessed=8 << 20, transcendentals=1 << 17),
    )(hidden_states, head_weight, teacher_index, teacher_logits, loss_weight)


def solution(mesh):
    in_specs = (
        P("dp", None),
        P("dp", "vocab"),
        P(("dp", "vocab"), None),
        P(("dp", "vocab"), None),
        P("dp"),
    )
    out_specs = (P("dp", "vocab"), P("dp", "vocab"))
    return jax.shard_map(local, mesh=mesh, in_specs=in_specs, out_specs=out_specs, check_vma=False)
```

time: 1230 us -> 144 us (0.12)
  the two profiles are of different devices: /device:TPU:2 before, /device:TPU:4 now
where the time goes in v1:
time: 144 us
  Pallas kernels  140 us (97%)
  local copies, waits for them, and re-layouts  3.71 us (3%)
    pallas_call x1, Pallas kernels, local(): pl.pallas_call(kernel, out_shape=(jax.ShapeDtypeStruct((DC, V), BF16), ja...  140 us

profile of v1, /device:TPU:4, one launch (start us, length us, event | category | flops | bytes accessed | tf_op | source)
XLA Modules:
  0.0 144.1 jit_solution(1868873368082833009)
XLA Ops:
  0.6 139.7 %shard_map.68 = (bf16[512,1024]{1,0:T(8,128)(2,1)}, bf16[128,64]{1,0:T(8,128)(2,1)}) custom-call(bf16[128,4096]{1,0:T(8,128)(2,1)} %h.1, bf16[512,1024]{1,0:T(8,128)(2,1)} %w.1, s32[2,64]{1,0:T(2,128)} %ti.1, f32[2,64]{1,0:T(2,128)} %tl.1, f32[128]{0:T(128)} %lw.1), custom_call_target="tpu_custom_call" | custom-call | flops 3221225472 | bytes 8388608 | tf_op jit(solution)/shard_map/pallas_call | solution.py:358
  140.3 1.4 %copy.7 = bf16[128,64]{0,1:T(8,128)(2,1)} copy(bf16[128,64]{1,0:T(8,128)(2,1)} %get-tuple-element.3) | data formatting | bytes 32768 | tf_op jit(solution)/shard_map/pallas_call | solution.py:358
  141.8 2.3 %copy.9 = bf16[512,1024]{1,0:T(8,128)(2,1)} copy(bf16[512,1024]{1,0:T(8,128)(2,1)} %get-tuple-element.6) | data formatting | bytes 2097152

commit v2 on v1

v2 whole, which is shorter than its diff:
```python
import functools

import jax
import jax.numpy as jnp
from jax import lax
from jax.experimental import pallas as pl
from jax.experimental.pallas import tpu as pltpu
from jax.sharding import PartitionSpec as P

MESH = pl.DeviceIdType.MESH
F32 = jnp.float32
BF16 = jnp.bfloat16

NX, NY, NZ = 4, 4, 16
TOK = 128
D = 4096
DX = D // NX
DC = DX // 2
V = 1024
ZZ = NZ // NX
DZ = DX // ZZ
DY = DZ // NY
K = 64
HD = F32
ZD = F32


def dot(a, b, ca, cb):
    return lax.dot_general(a, b, (((ca,), (cb,)), ((), ())), preferred_element_type=F32)


def kernel(
    h, w, ti_h, tl_h, lw_h, head_h, hid_o,
    ti, tl, lw, head_o, wn, wt, feat, feat_t, feat_o, part, fin_l, rel_l, tgt, g, go, acc_h,
    hf, hs, yrel, yfin, xs, za, zs, fin, tea, tez, tet, sty, stz,
    ss, rs, ls, fs, fr,
):
    dp, vo = lax.axis_index("dp"), lax.axis_index("vocab")
    x, c = dp // 2, dp % 2
    z, y = vo // NY, vo % NY
    zg, zl = z // ZZ, z % ZZ
    yp, y2, ym = (y + 1) % NY, (y + 2) % NY, (y + 3) % NY

    def at(xx, cc, zz, yy):
        return (xx * 2 + cc, zz * NY + yy)

    to_x = [None] + [at((x + r) % NX, c, z, y) for r in range(1, NX)]
    to_y = [None] + [at(x, c, z, (y + r) % NY) for r in range(1, NY)]
    to_zl = [None] + [at(x, c, zg * ZZ + (zl + r) % ZZ, y) for r in range(1, ZZ)]
    to_z = [None] + [at(x, c, (z + r) % NZ, y) for r in range(1, NZ)]
    mate = at(x, 1 - c, z, y)

    count = [0]
    sent = []

    def send(src, dst, dev):
        i = count[0]
        count[0] += 1
        d = pltpu.make_async_remote_copy(src, dst, ss.at[i], rs.at[i], device_id=dev, device_id_type=MESH)
        d.start()
        sent.append(d)
        return d

    own_w = pltpu.make_async_copy(w, wn.at[c], ls.at[0])
    own_w.start()
    own_h = pltpu.make_async_copy(h.at[:, pl.ds(pl.multiple_of(x * DX, DX), DX)], feat.at[0], ls.at[1])
    own_h.start()
    small = [
        pltpu.make_async_copy(src, dst, ls.at[2 + i])
        for i, (src, dst) in enumerate(((ti_h, ti), (tl_h, tl), (lw_h, lw)))
    ]
    for d in small:
        d.start()

    barrier = pltpu.get_barrier_semaphore()
    peers = to_x[1:] + [mate] + to_y[1:] + to_z[1:]
    for dev in peers:
        pl.semaphore_signal(barrier, inc=1, device_id=dev, device_id_type=MESH)

    def transpose_w(core):
        def body(i, carry):
            rows = pl.ds(pl.multiple_of(i * 128, 128), 128)
            wt[rows, pl.ds(pl.multiple_of(core * DC, DC), DC)] = wn[core, :, rows].T
            return carry

        lax.fori_loop(0, V // 128, body, 0)

    own_w.wait()
    transpose_w(c)
    for d in small:
        d.wait()
    pl.semaphore_wait(barrier, len(peers))

    def cols_of(r):
        return pl.ds(pl.multiple_of((x + r) % NX * DX, DX), DX)

    tq = TOK // NY
    quarter = pl.ds(pl.multiple_of(y * tq, tq), tq)
    th = TOK // 2
    pair = pl.ds(pl.multiple_of(z % 2 * th, th), th)
    zpeer = at(x, c, z + 1 - 2 * (z % 2), y)
    d_f2 = send(h.at[quarter, cols_of(2)], feat.at[2, quarter], to_x[2])
    d_f3 = send(h.at[pair, cols_of(1)], feat.at[3, pair], to_x[1])
    d_f1 = send(h.at[pair, cols_of(3)], feat.at[1, pair], to_x[3])
    d_w = send(w, wn.at[c], mate)

    row = lax.broadcasted_iota(jnp.int32, (8, 128), 0)
    mine = jnp.concatenate([ti[...].astype(F32), tl[...]], axis=1)
    mine = jnp.concatenate([mine] * 4, axis=0)
    tea[0] = jnp.where(row // 2 == y, mine, 0.0)
    d_tea = [send(tea.at[0], tea.at[NY - r], to_y[r]) for r in range(1, NY)]

    d_f2.wait_recv()
    d_f2y = [send(feat.at[2, quarter], feat.at[2, quarter], to_y[r]) for r in (2, 1, 3)]
    d_f1.wait_recv()
    d_f1z = send(feat.at[1, pair], feat.at[1, pair], zpeer)
    d_f3.wait_recv()
    d_f3z = send(feat.at[3, pair], feat.at[3, pair], zpeer)
    d_w.wait_recv()
    transpose_w(1 - c)

    def partial(r, lo, hi):
        feat_t[r] = feat[r].T

        def body(i, carry):
            rows = pl.ds(pl.multiple_of(i * 256, 256), 256)
            part[r, rows, :] = dot(wt[rows, :], feat_t[r], 1, 0)
            return carry

        lax.fori_loop(lo // 256, hi // 256, body, 0)

    half = V // 2
    top, bot = pl.ds(0, half), pl.ds(half, half)
    for d in d_f2y:
        d.wait_recv()
    partial(2, 0, V)
    r_top = send(part.at[2, top], rel_l.at[0], to_x[3])
    r_bot = send(part.at[2, bot], rel_l.at[1], to_x[1])
    d_f1z.wait_recv()
    partial(1, 0, V)
    a_p = send(part.at[1, top], fin_l.at[0, top], to_x[1])
    d_f3z.wait_recv()
    partial(3, 0, V)
    a_m = send(part.at[3, bot], fin_l.at[1, bot], to_x[3])
    for d in d_tea:
        d.wait_recv()
    tez[0] = tea[0] + tea[1] + tea[2] + tea[3]
    far = sorted(range(1, NZ), key=lambda r: -min(r, NZ - r))
    d_tez = [None] + [send(tez.at[0], tez.at[NZ - r], to_z[r]) for r in far]
    own_h.wait()
    d_fo = []
    r_bot.wait_recv()
    part[1, bot, :] += rel_l[1]
    b_p = send(part.at[1, bot], fin_l.at[0, bot], to_x[1])
    r_top.wait_recv()
    part[3, top, :] += rel_l[0]
    b_m = send(part.at[3, top], fin_l.at[1, top], to_x[3])
    partial(0, 0, V)
    for r in range(NX):
        rows = pl.ds(pl.multiple_of((1 - c) * DC, DC), DC)
        d_fo.append(send(feat_t.at[r, rows], feat_o.at[r], mate))

    for d in d_tez[1:]:
        d.wait_recv()
    for r in range(NZ):
        tet[pl.ds(pl.multiple_of(((z + r) % NZ) * 8, 8), 8), :] = tez[r]
    tt = tet[...].T
    tlog = tt[K:, :]
    texp = jnp.exp(tlog - jnp.max(tlog, axis=0, keepdims=True))
    lwr = lw[...].reshape(1, TOK)
    tet[pl.ds(K, K), :] = texp / jnp.sum(texp, axis=0, keepdims=True) * lwr
    tet[pl.ds(0, K), :] = tt[:K, :] - (vo * V).astype(F32)

    def dense(i, carry):
        base = pl.multiple_of(i * 128, 128)
        at_row = (lax.broadcasted_iota(jnp.int32, (128, TOK), 0) + base).astype(F32)
        acc = jnp.zeros((128, TOK), F32)
        for k in range(K):
            acc = jnp.where(at_row == tet[k : k + 1, :], tet[K + k : K + k + 1, :], acc)
        tgt[pl.ds(base, 128), :] = acc
        return carry

    lax.fori_loop(0, V // 128, dense, 0)

    for d in (a_p, a_m, b_p, b_m):
        d.wait_recv()
    logits = part[0] + (fin_l[0] + fin_l[1])
    m_loc = jnp.max(logits, axis=0, keepdims=True)
    p = jnp.exp(logits - m_loc)
    part[0] = p
    s_loc = jnp.sum(p, axis=0, keepdims=True)

    def exchange(buf, tos, m, s):
        n = len(tos)
        buf[0] = jnp.where(row[:2] == 0, m, s)
        far = sorted(range(1, n), key=lambda r: -min(r, n - r))
        ds = [send(buf.at[0], buf.at[n - r], tos[r]) for r in far]
        for d in ds:
            d.wait_recv()
        ms = [buf[r, 0:1, :] for r in range(n)]
        mm = functools.reduce(jnp.maximum, ms)
        return mm, sum(buf[r, 1:2, :] * jnp.exp(ms[r] - mm) for r in range(n))

    m_y, s_y = exchange(sty, to_y, m_loc, s_loc)
    m_all, s_all = exchange(stz, to_z, m_y, s_y)
    scale = lwr * jnp.exp(m_loc - m_all) / s_all
    g[0] = (part[0] * scale - tgt[...]).astype(BF16)

    gp_b = send(g.at[0, bot], g.at[3, bot], to_x[1])
    gm_t = send(g.at[0, top], g.at[1, top], to_x[3])
    gp_t = send(g.at[0, top], g.at[3, top], to_x[1])
    gm_b = send(g.at[0, bot], g.at[1, bot], to_x[3])
    d_go = [send(g.at[0], go.at[0], mate)]

    hrow = DZ // 2 * 2
    ht, hb = pl.ds(0, hrow // 2), pl.ds(hrow // 2, hrow // 2)
    pieces = {}

    def hidden(r):
        for q in range(ZZ):
            rows = q * DZ
            v = dot(wn[rows // DC, rows % DC : rows % DC + DZ, :], g[r], 1, 0)
            for yy in range(NY):
                hf[r, yy, q * DY : (q + 1) * DY, :] = v[yy * DY : (yy + 1) * DY]
        if HD == F32:
            src = hf
        else:
            hs[r] = hf[r].astype(HD)
            src = hs
        rt = send(src.at[r, y2, ht], yrel.at[r, 0], to_y[3])
        rb = send(src.at[r, y2, hb], yrel.at[r, 1], to_y[1])
        pt = send(src.at[r, yp, ht], yfin.at[r, 0, ht], to_y[1])
        mb = send(src.at[r, ym, hb], yfin.at[r, 1, hb], to_y[3])
        pieces[r] = [rt, rb, pt, mb]

    def relay(r):
        src = hf if HD == F32 else hs
        rt, rb, pt, mb = pieces[r]
        rb.wait_recv()
        src[r, yp, hb, :] = (hf[r, yp, hb, :] + yrel[r, 1].astype(F32)).astype(HD)
        pb = send(src.at[r, yp, hb], yfin.at[r, 0, hb], to_y[1])
        rt.wait_recv()
        src[r, ym, ht, :] = (hf[r, ym, ht, :] + yrel[r, 0].astype(F32)).astype(HD)
        mt = send(src.at[r, ym, ht], yfin.at[r, 1, ht], to_y[3])
        pieces[r] = [pt, mb, pb, mt]

    d_za = [None] * NX
    d_fin = []

    def rows_of(q):
        return pl.ds(pl.multiple_of((zl + q) % ZZ * DY, DY), DY)

    def level_a(r):
        for d in pieces[r]:
            d.wait_recv()
        xs[r] = (hf[r, y] + (yfin[r, 0].astype(F32) + yfin[r, 1].astype(F32))).astype(ZD)
        d_za[r] = [send(xs.at[r, rows_of(q)], za.at[r, ZZ - q], to_zl[q]) for q in (2, 1, 3)]

    def level_b(r):
        for d in d_za[r]:
            d.wait_recv()
        v = xs[r, rows_of(0), :].astype(F32)
        for q in range(1, ZZ):
            v += za[r, q].astype(F32)
        zs[r] = v.astype(ZD)
        d = pltpu.make_async_remote_copy(
            zs.at[r], fin.at[zg], fs.at[r], fr.at[zg],
            device_id=at((x + r) % NX, c, x * ZZ + zl, y), device_id_type=MESH,
        )
        d_fin.append(d)
        if r:
            d.start()
        else:

            @pl.when(zg != x)
            def _():
                d.start()

            @pl.when(zg == x)
            def _():
                fin[zg] = zs[0]

    def head(blocks, first, last):
        def body(i, carry):
            rows = pl.ds(pl.multiple_of(i // 4 * 256, 256), 256)
            cols = pl.ds(pl.multiple_of(i % 4 * 256, 256), 256)
            acc = None if first else acc_h[rows, cols]
            for r in blocks:
                mine = pl.ds(pl.multiple_of(c * DC + i // 4 * 256, 256), 256)
                for f, gr in ((feat_t[r, mine, :], g), (feat_o[r, rows, :], go)):
                    v = dot(f, gr[r, cols, :], 1, 1)
                    acc = v if acc is None else acc + v
            if last:
                head_o[rows, cols] = acc.astype(BF16)
            else:
                acc_h[rows, cols] = acc
            return carry

        lax.fori_loop(0, (DC // 256) * (V // 256), body, 0)

    hidden(0)
    gp_b.wait_recv()
    g2_b = send(g.at[3, bot], g.at[2, bot], to_x[1])
    gm_t.wait_recv()
    g2_t = send(g.at[1, top], g.at[2, top], to_x[3])
    gp_t.wait_recv()
    d_go.append(send(g.at[3], go.at[3], mate))
    hidden(3)
    relay(0)
    gm_b.wait_recv()
    d_go.append(send(g.at[1], go.at[1], mate))
    hidden(1)
    relay(3)
    g2_b.wait_recv()
    g2_t.wait_recv()
    d_go.append(send(g.at[2], go.at[2], mate))
    hidden(2)
    level_a(0)
    relay(1)
    level_a(3)
    for d in d_fo + d_go[:3]:
        d.wait_recv()
    head((0, 3, 1), True, False)
    relay(2)
    level_a(1)
    level_b(0)
    level_b(3)
    level_b(1)
    level_a(2)
    level_b(2)
    d_go[3].wait_recv()
    head((2,), False, True)
    out = pltpu.make_async_copy(head_o, head_h, ls.at[5])
    out.start()
    for q in range(NX):
        d = pltpu.make_async_remote_copy(
            zs.at[0], fin.at[q], fs.at[0], fr.at[q], device_id=mate, device_id_type=MESH
        )

        @pl.when((zg != x) | (zg != q))
        def _(d=d):
            d.wait_recv()

    total = fin[0].astype(F32)
    for q in range(1, NX):
        total += fin[q].astype(F32)
    hid_o[...] = total.astype(BF16)

    for d in sent:
        d.wait_send()
    out.wait()
    @pl.when(zg != x)
    def _():
        d_fin[0].wait_send()

    for d in d_fin[1:]:
        d.wait_send()


def local(hidden_states, head_weight, teacher_index, teacher_logits, loss_weight):
    vm = pl.BlockSpec(memory_space=pltpu.VMEM)
    anym = pl.BlockSpec(memory_space=pl.ANY)
    n_sems = 128
    scratch = [
        pltpu.VMEM((2, K), jnp.int32),
        pltpu.VMEM((2, K), F32),
        pltpu.VMEM((TOK,), F32),
        pltpu.VMEM((DC, V), BF16),
        pltpu.VMEM((2, DC, V), BF16),
        pltpu.VMEM((V, DX), BF16),
        pltpu.VMEM((NX, TOK, DX), BF16),
        pltpu.VMEM((NX, DX, TOK), BF16),
        pltpu.VMEM((NX, DC, TOK), BF16),
        pltpu.VMEM((NX, V, TOK), F32),
        pltpu.VMEM((2, V, TOK), F32),
        pltpu.VMEM((2, V // 2, TOK), F32),
        pltpu.VMEM((V, TOK), F32),
        pltpu.VMEM((NX, V, TOK), BF16),
        pltpu.VMEM((NX, V, TOK), BF16),
        pltpu.VMEM((DC, V), F32),
        pltpu.VMEM((NX, NY, DZ, TOK), F32),
        pltpu.VMEM((NX, NY, DZ, TOK) if HD != F32 else (1, 1, 8, TOK), HD),
        pltpu.VMEM((NX, 2, DZ // 2, TOK), HD),
        pltpu.VMEM((NX, 2, DZ, TOK), HD),
        pltpu.VMEM((NX, DZ, TOK), ZD),
        pltpu.VMEM((NX, ZZ, DY, TOK), ZD),
        pltpu.VMEM((NX, DY, TOK), ZD),
        pltpu.VMEM((NX, DY, TOK), ZD),
        pltpu.VMEM((NY, 8, 128), F32),
        pltpu.VMEM((NZ, 8, 128), F32),
        pltpu.VMEM((128, 128), F32),
        pltpu.VMEM((NY, 2, 128), F32),
        pltpu.VMEM((NZ, 2, 128), F32),
        pltpu.SemaphoreType.DMA((n_sems,)),
        pltpu.SemaphoreType.DMA((n_sems,)),
        pltpu.SemaphoreType.DMA((6,)),
        pltpu.SemaphoreType.DMA((NX,)),
        pltpu.SemaphoreType.DMA((NX,)),
    ]
    head_grad, hidden_grad = pl.pallas_call(
        kernel,
        out_shape=(
            jax.ShapeDtypeStruct((DC, V), BF16),
            jax.ShapeDtypeStruct((DY, TOK), BF16),
        ),
        in_specs=[anym] * 5,
        out_specs=(anym, vm),
        scratch_shapes=scratch,
        compiler_params=pltpu.CompilerParams(
            collective_id=0, has_side_effects=True, vmem_limit_bytes=56 * 1024 * 1024
        ),
        cost_estimate=pl.CostEstimate(flops=3 * 2 * 128 * 4096 * 1024, bytes_accessed=8 << 20, transcendentals=1 << 17),
    )(hidden_states, head_weight, teacher_index, teacher_logits, loss_weight)
    return head_grad, hidden_grad.T


def solution(mesh):
    in_specs = (
        P("dp", None),
        P("dp", "vocab"),
        P(("dp", "vocab"), None),
        P(("dp", "vocab"), None),
        P("dp"),
    )
    out_specs = (P("dp", "vocab"), P("dp", "vocab"))
    return jax.shard_map(local, mesh=mesh, in_specs=in_specs, out_specs=out_specs, check_vma=False)
```

time: 144 us -> 102 us (0.71)
  Pallas kernels: 140 us -> 98 us
    pallas_call x1, Pallas kernels: 140 us -> 98 us  [local(): pl.pallas_call(kernel, out_shape=(jax.ShapeDtypeStruct((DC, V), BF16), ja...]
    pallas_call x1 -> x0, local copies, waits for them, and re-layouts: 1.45 us -> none  [local(): pl.pallas_call(kernel, out_shape=(jax.ShapeDtypeStruct((DC, V), BF16), ja...]
where the time goes in v2:
time: 102 us
  Pallas kernels  98 us (96%)
  local copies, waits for them, and re-layouts  2.88 us (3%)
    pallas_call x1, Pallas kernels, local(): pl.pallas_call(kernel, out_shape=(jax.ShapeDtypeStruct((DC, V), BF16), ja...  98 us
    unnamed x4, local copies, waits for them, and re-layouts  2.88 us

profile of v2, /device:TPU:4, one launch (start us, length us, event | category | flops | bytes accessed | tf_op | source)
XLA Modules:
  0.0 101.5 jit_solution(5583625042296793596)
XLA Ops:
  0.6 98.0 %shard_map.68 = (bf16[512,1024]{1,0:T(8,128)(2,1)}, bf16[64,128]{1,0:T(8,128)(2,1)}) custom-call(bf16[128,4096]{1,0:T(8,128)(2,1)} %h.1, bf16[512,1024]{1,0:T(8,128)(2,1)} %w.1, s32[2,64]{1,0:T(2,128)} %ti_h.1, f32[2,64]{1,0:T(2,128)} %tl_h.1, f32[128]{0:T(128)} %lw_h.1), custom_call_target="tpu_custom_call" | custom-call | flops 3221225472 | bytes 8388608 | tf_op jit(solution)/shard_map/pallas_call | solution.py:400
  98.7 0.0 copy-start
  98.7 2.3 %copy.9 = bf16[512,1024]{1,0:T(8,128)(2,1)} copy(bf16[512,1024]{1,0:T(8,128)(2,1)} %get-tuple-element.8) | data formatting | bytes 2097152
  100.9 0.0 copy-done
  100.9 0.6 copy.10
Async XLA Ops:
  98.7 2.3 %copy-start = (bf16[64,128]{1,0:T(8,128)(2,1)S(1)}, bf16[64,128]{1,0:T(8,128)(2,1)}, u32[]{:S(2)}) copy-start(bf16[64,128]{1,0:T(8,128)(2,1)} %get-tuple-element.5) | copy-start | bytes 49156

commit v3 on v2

--- a/solution.py
+++ b/solution.py
@@ -21,8 +21,8 @@
 DZ = DX // ZZ
 DY = DZ // NY
 K = 64
-HD = F32
-ZD = F32
+HD = BF16
+ZD = BF16
 
 
 def dot(a, b, ca, cb):
@@ -30,8 +30,8 @@
 
 
 def kernel(
-    h, w, ti_h, tl_h, lw_h, head_h, hid_o,
-    ti, tl, lw, head_o, wn, wt, feat, feat_t, feat_o, part, fin_l, rel_l, tgt, g, go, acc_h,
+    h, w, ti_h, tl_h, lw_h, head_o, hid_o,
+    ti, tl, lw, wn, wt, feat, feat_t, feat_o, part, fin_l, rel_l, tgt, g, go, acc_h,
     hf, hs, yrel, yfin, xs, za, zs, fin, tea, tez, tet, sty, stz,
     ss, rs, ls, fs, fr,
 ):
@@ -208,9 +208,6 @@
 
     gp_b = send(g.at[0, bot], g.at[3, bot], to_x[1])
     gm_t = send(g.at[0, top], g.at[1, top], to_x[3])
-    gp_t = send(g.at[0, top], g.at[3, top], to_x[1])
-    gm_b = send(g.at[0, bot], g.at[1, bot], to_x[3])
-    d_go = [send(g.at[0], go.at[0], mate)]
 
     hrow = DZ // 2 * 2
     ht, hb = pl.ds(0, hrow // 2), pl.ds(hrow // 2, hrow // 2)
@@ -299,6 +296,9 @@
         lax.fori_loop(0, (DC // 256) * (V // 256), body, 0)
 
     hidden(0)
+    gp_t = send(g.at[0, top], g.at[3, top], to_x[1])
+    gm_b = send(g.at[0, bot], g.at[1, bot], to_x[3])
+    d_go = [send(g.at[0], go.at[0], mate)]
     gp_b.wait_recv()
     g2_b = send(g.at[3, bot], g.at[2, bot], to_x[1])
     gm_t.wait_recv()
@@ -330,8 +330,6 @@
     level_b(2)
     d_go[3].wait_recv()
     head((2,), False, True)
-    out = pltpu.make_async_copy(head_o, head_h, ls.at[5])
-    out.start()
     for q in range(NX):
         d = pltpu.make_async_remote_copy(
             zs.at[0], fin.at[q], fs.at[0], fr.at[q], device_id=mate, device_id_type=MESH
@@ -348,7 +346,6 @@
 
     for d in sent:
         d.wait_send()
-    out.wait()
     @pl.when(zg != x)
     def _():
         d_fin[0].wait_send()
@@ -365,7 +362,6 @@
         pltpu.VMEM((2, K), jnp.int32),
         pltpu.VMEM((2, K), F32),
         pltpu.VMEM((TOK,), F32),
-        pltpu.VMEM((DC, V), BF16),
         pltpu.VMEM((2, DC, V), BF16),
         pltpu.VMEM((V, DX), BF16),
         pltpu.VMEM((NX, TOK, DX), BF16),
@@ -393,18 +389,18 @@
         pltpu.VMEM((NZ, 2, 128), F32),
         pltpu.SemaphoreType.DMA((n_sems,)),
         pltpu.SemaphoreType.DMA((n_sems,)),
-        pltpu.SemaphoreType.DMA((6,)),
+        pltpu.SemaphoreType.DMA((5,)),
         pltpu.SemaphoreType.DMA((NX,)),
         pltpu.SemaphoreType.DMA((NX,)),
     ]
     head_grad, hidden_grad = pl.pallas_call(
         kernel,
         out_shape=(
-            jax.ShapeDtypeStruct((DC, V), BF16),
-            jax.ShapeDtypeStruct((DY, TOK), BF16),
+            pltpu.VMEM((DC, V), BF16),
+            pltpu.VMEM((DY, TOK), BF16),
         ),
         in_specs=[anym] * 5,
-        out_specs=(anym, vm),
+        out_specs=(vm, vm),
         scratch_shapes=scratch,
         compiler_params=pltpu.CompilerParams(
             collective_id=0, has_side_effects=True, vmem_limit_bytes=56 * 1024 * 1024

time: 102 us -> 91.6 us (0.90)
  Pallas kernels: 98 us -> 89.2 us
  local copies, waits for them, and re-layouts: 2.88 us -> 1.58 us
    pallas_call x1, Pallas kernels: 98 us -> 89.2 us  [local(): pl.pallas_call(kernel, out_shape=(pltpu.VMEM((DC, V), BF16), pltpu.VMEM((...]
    unnamed x4 -> x2, local copies, waits for them, and re-layouts: 2.88 us -> 1.58 us
where the time goes in v3:
time: 91.6 us; the launch traced here: 91.4 us
  Pallas kernels  89.2 us (97%)
  local copies, waits for them, and re-layouts  1.58 us (2%)
    pallas_call x1, Pallas kernels, local(): pl.pallas_call(kernel, out_shape=(pltpu.VMEM((DC, V), BF16), pltpu.VMEM((...  89.2 us

profile of v3, /device:TPU:4, one launch (start us, length us, event | category | flops | bytes accessed | tf_op | source)
XLA Modules:
  0.0 91.4 jit_solution(1028580360226472185)
XLA Ops:
  0.6 89.2 %shard_map.68 = (bf16[512,1024]{1,0:T(8,128)(2,1)S(1)}, bf16[64,128]{1,0:T(8,128)(2,1)S(1)}) custom-call(bf16[128,4096]{1,0:T(8,128)(2,1)} %h.1, bf16[512,1024]{1,0:T(8,128)(2,1)} %w.1, s32[2,64]{1,0:T(2,128)} %ti_h.1, f32[2,64]{1,0:T(2,128)} %tl_h.1, f32[128]{0:T(128)} %lw_h.1), custom_call_target="tpu_custom_call" | custom-call | flops 3221225472 | bytes 8388608 | tf_op jit(solution)/shard_map/pallas_call | solution.py:396
  89.9 1.0 %copy.9 = bf16[512,1024]{1,0:T(8,128)(2,1)} copy(bf16[512,1024]{1,0:T(8,128)(2,1)S(1)} %get-tuple-element.6) | data formatting | bytes 2097152
  90.8 0.6 copy.10

commit v4 on v3

--- a/solution.py
+++ b/solution.py
@@ -32,8 +32,8 @@
 def kernel(
     h, w, ti_h, tl_h, lw_h, head_o, hid_o,
     ti, tl, lw, wn, wt, feat, feat_t, feat_o, part, fin_l, rel_l, tgt, g, go, acc_h,
-    hf, hs, yrel, yfin, xs, za, zs, fin, tea, tez, tet, sty, stz,
-    ss, rs, ls, fs, fr,
+    hf, hs, yrel, yfin, xs, za, zs, fin, tea, tez, tet, stat,
+    ss, rs, ls, fs, fr, turn,
 ):
     dp, vo = lax.axis_index("dp"), lax.axis_index("vocab")
     x, c = dp // 2, dp % 2
@@ -60,6 +60,16 @@
         d.start()
         sent.append(d)
         return d
+
+    def my_turn(i):
+        @pl.when(c == 1)
+        def _():
+            pl.semaphore_wait(turn.at[i], 1)
+
+    def your_turn(i):
+        @pl.when(c == 0)
+        def _():
+            pl.semaphore_signal(turn.at[i], inc=1, device_id=mate, device_id_type=MESH)
 
     own_w = pltpu.make_async_copy(w, wn.at[c], ls.at[0])
     own_w.start()
@@ -134,6 +144,7 @@
     for d in d_f2y:
         d.wait_recv()
     partial(2, 0, V)
+    my_turn(1)
     r_top = send(part.at[2, top], rel_l.at[0], to_x[3])
     r_bot = send(part.at[2, bot], rel_l.at[1], to_x[1])
     d_f1z.wait_recv()
@@ -155,6 +166,7 @@
     r_top.wait_recv()
     part[3, top, :] += rel_l[0]
     b_m = send(part.at[3, top], fin_l.at[1, top], to_x[3])
+    your_turn(1)
     partial(0, 0, V)
     for r in range(NX):
         rows = pl.ds(pl.multiple_of((1 - c) * DC, DC), DC)
@@ -190,19 +202,18 @@
     part[0] = p
     s_loc = jnp.sum(p, axis=0, keepdims=True)
 
-    def exchange(buf, tos, m, s):
-        n = len(tos)
-        buf[0] = jnp.where(row[:2] == 0, m, s)
-        far = sorted(range(1, n), key=lambda r: -min(r, n - r))
-        ds = [send(buf.at[0], buf.at[n - r], tos[r]) for r in far]
-        for d in ds:
-            d.wait_recv()
-        ms = [buf[r, 0:1, :] for r in range(n)]
-        mm = functools.reduce(jnp.maximum, ms)
-        return mm, sum(buf[r, 1:2, :] * jnp.exp(ms[r] - mm) for r in range(n))
-
-    m_y, s_y = exchange(sty, to_y, m_loc, s_loc)
-    m_all, s_all = exchange(stz, to_z, m_y, s_y)
+    stat[0] = jnp.where(row[:2] == 0, m_loc, s_loc)
+    steps = [(rz, ry) for rz in range(NZ) for ry in range(NY) if rz or ry]
+    steps.sort(key=lambda s: -min(s[0], NZ - s[0]) - min(s[1], NY - s[1]))
+    d_st = []
+    for rz, ry in steps:
+        slot = (NZ - rz) % NZ * NY + (NY - ry) % NY
+        d_st.append(send(stat.at[0], stat.at[slot], at(x, c, (z + rz) % NZ, (y + ry) % NY)))
+    for d in d_st:
+        d.wait_recv()
+    ms = stat[:, 0, :]
+    m_all = jnp.max(ms, axis=0, keepdims=True)
+    s_all = jnp.sum(stat[:, 1, :] * jnp.exp(ms - m_all), axis=0, keepdims=True)
     scale = lwr * jnp.exp(m_loc - m_all) / s_all
     g[0] = (part[0] * scale - tgt[...]).astype(BF16)
 
@@ -277,17 +288,20 @@
             def _():
                 fin[zg] = zs[0]
 
-    def head(blocks, first, last):
+    def head(other):
         def body(i, carry):
             rows = pl.ds(pl.multiple_of(i // 4 * 256, 256), 256)
             cols = pl.ds(pl.multiple_of(i % 4 * 256, 256), 256)
-            acc = None if first else acc_h[rows, cols]
-            for r in blocks:
-                mine = pl.ds(pl.multiple_of(c * DC + i // 4 * 256, 256), 256)
-                for f, gr in ((feat_t[r, mine, :], g), (feat_o[r, rows, :], go)):
-                    v = dot(f, gr[r, cols, :], 1, 1)
-                    acc = v if acc is None else acc + v
-            if last:
+            if other:
+                f, gr, f_rows = feat_o, go, rows
+                acc = acc_h[rows, cols]
+            else:
+                f, gr, f_rows = feat_t, g, pl.ds(pl.multiple_of(c * DC + i // 4 * 256, 256), 256)
+                acc = None
+            for r in range(NX):
+                v = dot(f[r, f_rows, :], gr[r, cols, :], 1, 1)
+                acc = v if acc is None else acc + v
+            if other:
                 head_o[rows, cols] = acc.astype(BF16)
             else:
                 acc_h[rows, cols] = acc
@@ -318,18 +332,17 @@
     level_a(0)
     relay(1)
     level_a(3)
-    for d in d_fo + d_go[:3]:
-        d.wait_recv()
-    head((0, 3, 1), True, False)
     relay(2)
     level_a(1)
     level_b(0)
     level_b(3)
     level_b(1)
     level_a(2)
+    head(False)
     level_b(2)
-    d_go[3].wait_recv()
-    head((2,), False, True)
+    for d in d_fo + d_go:
+        d.wait_recv()
+    head(True)
     for q in range(NX):
         d = pltpu.make_async_remote_copy(
             zs.at[0], fin.at[q], fs.at[0], fr.at[q], device_id=mate, device_id_type=MESH
@@ -357,7 +370,7 @@
 def local(hidden_states, head_weight, teacher_index, teacher_logits, loss_weight):
     vm = pl.BlockSpec(memory_space=pltpu.VMEM)
     anym = pl.BlockSpec(memory_space=pl.ANY)
-    n_sems = 128
+    n_sems = 160
     scratch = [
         pltpu.VMEM((2, K), jnp.int32),
         pltpu.VMEM((2, K), F32),
@@ -385,13 +398,13 @@
         pltpu.VMEM((NY, 8, 128), F32),
         pltpu.VMEM((NZ, 8, 128), F32),
         pltpu.VMEM((128, 128), F32),
-        pltpu.VMEM((NY, 2, 128), F32),
-        pltpu.VMEM((NZ, 2, 128), F32),
+        pltpu.VMEM((NZ * NY, 2, 128), F32),
         pltpu.SemaphoreType.DMA((n_sems,)),
         pltpu.SemaphoreType.DMA((n_sems,)),
         pltpu.SemaphoreType.DMA((5,)),
         pltpu.SemaphoreType.DMA((NX,)),
         pltpu.SemaphoreType.DMA((NX,)),
+        pltpu.SemaphoreType.REGULAR((2,)),
     ]
     head_grad, hidden_grad = pl.pallas_call(
         kernel,

time: 91.6 us -> 88.4 us (0.965)
  Pallas kernels: 89.2 us -> 85.5 us
    pallas_call x1, Pallas kernels: 89.2 us -> 85.5 us  [local(): pl.pallas_call(kernel, out_shape=(pltpu.VMEM((DC, V), BF16), pltpu.VMEM((...]
where the time goes in v4:
time: 88.4 us; the launch traced here: 87.7 us
  Pallas kernels  85.5 us (97%)
  local copies, waits for them, and re-layouts  1.58 us (2%)
    pallas_call x1, Pallas kernels, local(): pl.pallas_call(kernel, out_shape=(pltpu.VMEM((DC, V), BF16), pltpu.VMEM((...  85.5 us

profile of v4, /device:TPU:4, one launch (start us, length us, event | category | flops | bytes accessed | tf_op | source)
XLA Modules:
  0.0 87.7 jit_solution(7417787162846435404)
XLA Ops:
  0.6 85.5 %shard_map.68 = (bf16[512,1024]{1,0:T(8,128)(2,1)S(1)}, bf16[64,128]{1,0:T(8,128)(2,1)S(1)}) custom-call(bf16[128,4096]{1,0:T(8,128)(2,1)} %h.1, bf16[512,1024]{1,0:T(8,128)(2,1)} %w.1, s32[2,64]{1,0:T(2,128)} %ti_h.1, f32[2,64]{1,0:T(2,128)} %tl_h.1, f32[128]{0:T(128)} %lw_h.1), custom_call_target="tpu_custom_call" | custom-call | flops 3221225472 | bytes 8388608 | tf_op jit(solution)/shard_map/pallas_call | solution.py:409
  86.2 1.0 %copy.9 = bf16[512,1024]{1,0:T(8,128)(2,1)} copy(bf16[512,1024]{1,0:T(8,128)(2,1)S(1)} %get-tuple-element.6) | data formatting | bytes 2097152
  87.1 0.6 copy.10

commit v5 on v4

--- a/solution.py
+++ b/solution.py
@@ -21,8 +21,8 @@
 DZ = DX // ZZ
 DY = DZ // NY
 K = 64
-HD = BF16
-ZD = BF16
+HD = F32
+ZD = F32
 
 
 def dot(a, b, ca, cb):

time: 88.4 us -> 101 us (1.14)
  the two profiles are of different devices: /device:TPU:4 before, /device:TPU:5 now
where the time goes in v5:
time: 101 us; the launch traced here: 100 us
  Pallas kernels  98.2 us (97%)
  local copies, waits for them, and re-layouts  1.58 us (2%)
    pallas_call x1, Pallas kernels, local(): pl.pallas_call(kernel, out_shape=(pltpu.VMEM((DC, V), BF16), pltpu.VMEM((...  98.2 us

profile of v5, /device:TPU:5, one launch (start us, length us, event | category | flops | bytes accessed | tf_op | source)
XLA Modules:
  0.0 100.4 jit_solution(3325794031943655785)
XLA Ops:
  0.6 98.2 %shard_map.68 = (bf16[512,1024]{1,0:T(8,128)(2,1)S(1)}, bf16[64,128]{1,0:T(8,128)(2,1)S(1)}) custom-call(bf16[128,4096]{1,0:T(8,128)(2,1)} %h.1, bf16[512,1024]{1,0:T(8,128)(2,1)} %w.1, s32[2,64]{1,0:T(2,128)} %ti_h.1, f32[2,64]{1,0:T(2,128)} %tl_h.1, f32[128]{0:T(128)} %lw_h.1), custom_call_target="tpu_custom_call" | custom-call | flops 3221225472 | bytes 8388608 | tf_op jit(solution)/shard_map/pallas_call | solution.py:409
  98.8 1.0 copy.9
  99.8 0.6 copy.10
